TPU v7x, 128 devices: a whole 4x4x4 slice. The times are simulated.
128 devices in a mesh: pat: 16 (over x, y), tile: 8 (over z, core).
Axes of the slice: x: 4, y: 4, z: 4, core: 2. Of those that a mesh axis runs over, the one named last changes fastest.
Arguments:
- scanned: int32 [32, 32], P('tile', 'pat'), may hold values from 0 to 1, as said below
- measured: float32 [32, 32, 256, 256], P('tile', 'pat'), may hold values from 0 to 2
- obj: float32 [2, 2, 4096, 4096], P(None, None, 'tile', 'pat'), may hold values from -5 to 5
- probe: float32 [2, 256, 256], replicated, may hold values from -6 to 6
Outputs:
- grad_obj: float32 [2, 2, 4096, 4096], P(None, None, 'tile', 'pat')
- grad_probe: float32 [2, 256, 256], replicated
Inputs may be any that keep to these rules, and one draw needn't show every extreme that they name: `scanned`: the grid points of rows 0 to 3 and columns 0 to 1 are all 1; the last grid row and the last grid column are all 0; the share of 1 may differ between groups of four grid rows.
All inputs are finite; a program needn't handle non-finite values.
Results may differ from a plain program's by a relative error of at most 0.0003.
Values sent between devices are 32-bit elements; how exact they have to be, the bound alone decides.
A program may use at most 128 MiB of HBM per device.

v0:
```python
import math

import jax
import jax.numpy as jnp
from jax import lax
from jax.sharding import PartitionSpec as P

PHASE_SCALE = 40.0


def passed_along(block, axis, distance):
    devices = range(lax.axis_size(axis))
    route = [(i - distance, i) for i in devices if i - distance in devices]
    return lax.ppermute(block, axis, route)


def propagator(size):
    index = jnp.arange(size, dtype=jnp.int32)
    signed = jnp.where(index < (size + 1) // 2, index, index - size).astype(jnp.float32) / size
    phase = PHASE_SCALE * (signed[:, None] ** 2 + signed[None, :] ** 2)
    return (jnp.cos(phase), -jnp.sin(phase))


def dft_tables(size):
    index = jnp.arange(size, dtype=jnp.int32)
    product = index[:, None] * index[None, :] % size
    angle = 2.0 * math.pi / size * product.astype(jnp.float32)
    scale = 1.0 / math.sqrt(size)
    return (jnp.cos(angle) * scale, -jnp.sin(angle) * scale)


def matmul(left, right):
    return jnp.dot(left, right, precision=lax.Precision.HIGHEST, preferred_element_type=jnp.float32)


def transform(real, imag, cos_t, sin_t):
    left_re = matmul(cos_t, real) - matmul(sin_t, imag)
    left_im = matmul(cos_t, imag) + matmul(sin_t, real)
    out_re = matmul(left_re, cos_t) - matmul(left_im, sin_t)
    out_im = matmul(left_re, sin_t) + matmul(left_im, cos_t)
    return (out_re, out_im)


def pattern_loss(window, probe, measured, tables):
    cos_t, sin_t, prop_re, prop_im = tables
    wave_re = probe[0] * window[0, 0] - probe[1] * window[0, 1]
    wave_im = probe[0] * window[0, 1] + probe[1] * window[0, 0]
    freq_re, freq_im = transform(wave_re, wave_im, cos_t, sin_t)
    freq_re, freq_im = (
        freq_re * prop_re - freq_im * prop_im,
        freq_re * prop_im + freq_im * prop_re,
    )
    back_re, back_im = transform(freq_re, freq_im, cos_t, -sin_t)
    wave_re = back_re * window[1, 0] - back_im * window[1, 1]
    wave_im = back_re * window[1, 1] + back_im * window[1, 0]
    far_re, far_im = transform(wave_re, wave_im, cos_t, sin_t)
    diff = far_re * far_re + far_im * far_im - measured
    return 0.5 * jnp.sum(diff * diff)


def process(windows, measured, live, probe, tables):
    count = windows.shape[0]

    def visit(index, totals):
        grads, probe_grads = totals

        def work(unused):
            return jax.grad(pattern_loss, argnums=(0, 1))(
                windows[index], probe, measured[index], tables
            )

        def skip(unused):
            return (jnp.zeros(windows.shape[1:], jnp.float32), jnp.zeros(probe.shape, jnp.float32))

        g_win, g_probe = lax.cond(live[index] > 0, work, skip, 0)
        return (grads.at[index].set(g_win), probe_grads.at[index].set(g_probe))

    init = (jnp.zeros(windows.shape, jnp.float32), jnp.zeros((count,) + probe.shape, jnp.float32))
    return lax.fori_loop(0, count, visit, init)


def on_device(scanned, measured, obj, probe):
    size = probe.shape[-1]
    step = size // 2
    rows_blk = obj.shape[2]
    cols_blk = obj.shape[3]
    grid_r, grid_c = scanned.shape
    slots = grid_r * grid_c
    cos_t, sin_t = dft_tables(size)
    prop_re, prop_im = propagator(size)
    tables = (cos_t, sin_t, prop_re, prop_im)
    right = passed_along(obj[:, :, :, :step], "pat", -1)
    wide = jnp.concatenate([obj, right], axis=3)
    below = passed_along(wide[:, :, :step, :], "tile", -1)
    padded = jnp.concatenate([wide, below], axis=2)
    windows = jnp.stack(
        [
            padded[:, :, a * step : a * step + size, b * step : b * step + size]
            for a in range(grid_r)
            for b in range(grid_c)
        ]
    )
    intensity = measured.reshape(slots, size, size)
    live = scanned.reshape(slots)
    win_grads, probe_each = process(windows, intensity, live, probe, tables)
    probe_local = jnp.sum(probe_each, axis=0)
    grad_pad = jnp.zeros(padded.shape, jnp.float32)
    for slot in range(slots):
        row, col = divmod(slot, grid_c)
        grad_pad = grad_pad.at[
            :, :, row * step : row * step + size, col * step : col * step + size
        ].add(win_grads[slot])
    lower = passed_along(grad_pad[:, :, rows_blk:, :], "tile", 1)
    grad_wide = grad_pad[:, :, :rows_blk, :].at[:, :, :step, :].add(lower)
    side = passed_along(grad_wide[:, :, :, cols_blk:], "pat", 1)
    grad_obj = grad_wide[:, :, :, :cols_blk].at[:, :, :, :step].add(side)
    grad_probe = lax.psum(probe_local, ("pat", "tile"))
    return (grad_obj, grad_probe)


def solution(mesh):
    in_specs = (P("tile", "pat"), P("tile", "pat", None, None), P(None, None, "tile", "pat"), P())
    out_specs = (P(None, None, "tile", "pat"), P())
    return jax.shard_map(
        on_device, mesh=mesh, in_specs=in_specs, out_specs=out_specs, check_vma=False
    )
```

profile of v0, /device:TPU:1, one launch (start us, length us, event | category | flops | bytes accessed | tf_op | source)
XLA Modules:
  0.0 676.5 jit_solution(1814385697405271686)
XLA Ops:
  15.6 20.7 %collective-permute-done = f32[2,2,512,128]{3,2,1,0:T(8,128)S(1)} collective-permute-done((f32[2,2,512,128]{3,2,1,0:T(8,128)}, f32[2,2,512,128]{3,2,1,0:T(8,128)S(1)}, u32[]{:S(2)}, u32[]{:S(2)}) %collective-permute-start) | collective-permute-done | bytes 1048608 | tf_op jit(solution)/shard_map/ppermute | solution.py:14
  36.6 3.5 collective-permute-start.1
  40.4 11.1 %collective-permute-done.1 = f32[2,2,128,384]{3,2,1,0:T(8,128)S(1)} collective-permute-done((f32[2,2,128,384]{3,2,1,0:T(8,128)S(1)}, f32[2,2,128,384]{3,2,1,0:T(8,128)S(1)}, u32[]{:S(2)}, u32[]{:S(2)}) %collective-permute-start.1) | collective-permute-done | bytes 786464 | tf_op jit(solution)/shard_map/ppermute | solution.py:14
  51.7 3.2 copy-done.5
  54.9 4.2 broadcast_in_dim.52
  61.5 166.5 %while.30 = (s32[]{:T(128)}, f32[8,2,2,256,256]{4,3,2,1,0:T(8,128)}, f32[8,2,256,256]{3,2,1,0:T(8,128)}, s32[8]{0:T(128)S(1)}, f32[2,256,256]{2,1,0:T(8,128)S(1)...) while((s32[]{:T(128)}, ...), condition=%wide.region_5.6_spmd.clone.clone.clone, body=%wide.region_0.5_spmd.clone.clone.clone.sunk | while | flops 9673703424 | bytes 73403840 | solution.py:79
  84.1 3.1 select_dynamic-update-slice_fusion.4
  92.8 3.0 select_dynamic-update-slice_fusion.4
  100.4 38.9 %conditional.5 = (f32[1,2,2,256,256]{4,3,2,1,0:T(8,128)S(1)}, f32[1,2,256,256]{3,2,1,0:T(8,128)S(1)}) conditional(s32[]{:T(128)} %bitcast.281, () %tuple.200, (f32[2,256,256]{2,1,0:T(8,128)S(1)}, s32[]{:T(128)}, f32[8,2,2,256,256]{4,3,2,1,0:T(8,128)}, f32[256,256]{1,0:T(8,128)S(1)}, f32[256,256]{1,0:T(8,128)S(1)}, ...), branch_computations={%region_2.2_spmd, %region_3.3_spmd.clone} | conditional | flops 9672261632 | bytes 67895408 | solution.py:75
  140.1 3.0 select_dynamic-update-slice_fusion.4
  148.7 3.0 select_dynamic-update-slice_fusion.4
  157.3 3.1 select_dynamic-update-slice_fusion.4
  165.0 38.9 %conditional.5 = (f32[1,2,2,256,256]{4,3,2,1,0:T(8,128)S(1)}, f32[1,2,256,256]{3,2,1,0:T(8,128)S(1)}) conditional(s32[]{:T(128)} %bitcast.281, () %tuple.200, (f32[2,256,256]{2,1,0:T(8,128)S(1)}, s32[]{:T(128)}, f32[8,2,2,256,256]{4,3,2,1,0:T(8,128)}, f32[256,256]{1,0:T(8,128)S(1)}, f32[256,256]{1,0:T(8,128)S(1)}, ...), branch_computations={%region_2.2_spmd, %region_3.3_spmd.clone} | conditional | flops 9672261632 | bytes 67895408 | solution.py:75
  204.7 3.0 select_dynamic-update-slice_fusion.4
  213.3 3.0 select_dynamic-update-slice_fusion.4
  221.8 3.0 select_dynamic-update-slice_fusion.4
  231.5 3.4 add_select_fusion.1
  234.9 11.1 %scatter-add.35 = f32[2,2,640,384]{3,2,1,0:T(8,128)} dynamic-update-slice(f32[2,2,640,384]{3,2,1,0:T(8,128)} %scatter-add.34, f32[2,2,256,256]{3,2,1,0:T(8,128)S(1)} %add_select_fusion.1, s32[]{:T(128)} %constant.425.clone.1, s32[]{:T(128)} %constant.425.clone.1, s32[]{:T(128)} %bitcast.38, s32[]{:T(128)} %bitcast.39) | dynamic-update-slice | bytes 2097156 | tf_op jit(solution)/shard_map/scatter-add | solution.py:112
  254.1 2.7 fusion.49
  263.4 195.7 %collective-permute-start.2 = (f32[2,2,128,384]{3,2,1,0:T(8,128)S(1)}, f32[2,2,128,384]{3,2,1,0:T(8,128)S(1)}, u32[]{:S(2)}, u32[]{:S(2)}) collective-permute-start(f32[2,2,128,384]{3,2,1,0:T(8,128)S(1)} %slice.575), channel_id=1, source_target_pairs={{0,1},{1,2},{2,3},{3,4},{4,5},{5,6},{6,7},{8,9},{9,10},{10,11},{11... | collective-permute-start | bytes 2359304 | tf_op jit(solution)/shard_map/ppermute | solution.py:14
  461.2 28.9 %collective-permute-done.2 = f32[2,2,128,384]{3,2,1,0:T(8,128)S(1)} collective-permute-done((f32[2,2,128,384]{3,2,1,0:T(8,128)S(1)}, f32[2,2,128,384]{3,2,1,0:T(8,128)S(1)}, u32[]{:S(2)}, u32[]{:S(2)}) %collective-permute-start.2) | collective-permute-done | bytes 786464 | tf_op jit(solution)/shard_map/ppermute | solution.py:14
  495.3 3.3 reduce_sum.9
  500.4 17.6 %collective-permute-done.3 = f32[2,2,512,128]{3,2,1,0:T(8,128)S(1)} collective-permute-done((f32[2,2,512,128]{3,2,1,0:T(8,128)}, f32[2,2,512,128]{3,2,1,0:T(8,128)S(1)}, u32[]{:S(2)}, u32[]{:S(2)}) %collective-permute-start.3) | collective-permute-done | bytes 1048608 | tf_op jit(solution)/shard_map/ppermute | solution.py:14
  519.4 148.0 %all-reduce.15.cloned.1.call-done = f32[2,256,256]{2,1,0:T(8,128)} async-done(((f32[2,256,256]{2,1,0:T(8,128)}), f32[2,256,256]{2,1,0:T(8,128)}) %all-reduce.15.cloned.1.call-update) | async-done | bytes 524304 | tf_op jit(solution)/shard_map/psum | solution.py:117
  (244 shorter events, 158.4 us)
Async XLA Ops:
  7.2 8.3 %copy-start.3 = (f32[2,2,512,256]{3,2,1,0:T(8,128)S(1)}, f32[2,2,512,256]{3,2,1,0:T(8,128)}, u32[]{:S(2)}) copy-start(f32[2,2,512,256]{3,2,1,0:T(8,128)} %param.34) | copy-start | bytes 6291460
  7.2 660.2 %all-reduce.15.cloned.1.call-start = ((), (), s32[]{:S(2)}) async-start(), calls=%async_computation | async-start | bytes 1048576 | tf_op jit(solution)/shard_map/psum | solution.py:117
  9.6 26.7 %collective-permute-start = (f32[2,2,512,128]{3,2,1,0:T(8,128)}, f32[2,2,512,128]{3,2,1,0:T(8,128)S(1)}, u32[]{:S(2)}, u32[]{:S(2)}) collective-permute-start(f32[2,2,512,128]{3,2,1,0:T(8,128)} %slice.522), channel_id=1, source_target_pairs={{8,0},{16,8},{24,16},{32,24},{40,32},{48,40},{56,48},{64,56},{72,6... | collective-permute-start | bytes 3145736 | tf_op jit(solution)/shard_map/ppermute | solution.py:14
  36.6 14.9 %collective-permute-start.1 = (f32[2,2,128,384]{3,2,1,0:T(8,128)S(1)}, f32[2,2,128,384]{3,2,1,0:T(8,128)S(1)}, u32[]{:S(2)}, u32[]{:S(2)}) collective-permute-start(f32[2,2,128,384]{3,2,1,0:T(8,128)S(1)} %slice.566), channel_id=1, source_target_pairs={{1,0},{2,1},{3,2},{4,3},{5,4},{6,5},{7,6},{9,8},{10,9},{11,10},{12... | collective-permute-start | bytes 2359304 | tf_op jit(solution)/shard_map/ppermute | solution.py:14
  51.7 3.2 copy-start.5
  59.1 2.4 copy-start
  59.2 2.4 copy-start.7
  59.2 2.4 copy-start.8
  136.7 2.6 copy-start.1
  136.7 2.6 copy-start.2
  201.3 2.6 copy-start.1
  201.3 2.6 copy-start.2
  263.4 226.7 %collective-permute-start.2 = (f32[2,2,128,384]{3,2,1,0:T(8,128)S(1)}, f32[2,2,128,384]{3,2,1,0:T(8,128)S(1)}, u32[]{:S(2)}, u32[]{:S(2)}) collective-permute-start(f32[2,2,128,384]{3,2,1,0:T(8,128)S(1)} %slice.575), channel_id=1, source_target_pairs={{0,1},{1,2},{2,3},{3,4},{4,5},{5,6},{6,7},{8,9},{9,10},{10,11},{11... | collective-permute-start | bytes 2359304 | tf_op jit(solution)/shard_map/ppermute | solution.py:14
  491.3 1.6 copy-start.4
  494.0 24.0 %collective-permute-start.3 = (f32[2,2,512,128]{3,2,1,0:T(8,128)}, f32[2,2,512,128]{3,2,1,0:T(8,128)S(1)}, u32[]{:S(2)}, u32[]{:S(2)}) collective-permute-start(f32[2,2,512,128]{3,2,1,0:T(8,128)} %slice.578), channel_id=1, source_target_pairs={{0,8},{8,16},{16,24},{24,32},{32,40},{40,48},{48,56},{56,64},{64,7... | collective-permute-start | bytes 3145736 | tf_op jit(solution)/shard_map/ppermute | solution.py:14
  519.4 149.9 %copy-start.6 = (f32[2,2,512,256]{3,2,1,0:T(8,128)}, f32[2,2,512,256]{3,2,1,0:T(8,128)S(1)}, u32[]{:S(2)}) copy-start(f32[2,2,512,256]{3,2,1,0:T(8,128)S(1)} %fusion.46) | copy-start | bytes 6291460
Sparse Core Ops, SparseCore 0:
  498.8 168.5 all-reduce.14
where the time goes:
time: 682 us; the launch traced here: 676 us
  waiting for transfers between devices  226 us (33%)
  starting transfers between devices  202 us (30%)
  other arithmetic  87.8 us (13%)
  matrix products  65.2 us (10%)
  local copies, waits for them, and re-layouts  54 us (8%)
  loops' own time  26.7 us (4%)
  between operations  14.6 us (2%)
    ppermute x4, starting transfers between devices, passed_along(): return lax.ppermute(block, axis, route)  202 us
    psum x1, waiting for transfers between devices, on_device(): grad_probe = lax.psum(probe_local, ('pat', 'tile'))  148 us
    ppermute x4, waiting for transfers between devices, passed_along(): return lax.ppermute(block, axis, route)  78.3 us
    dot_general x96, matrix products, matmul(): jnp.dot(left, right, precision=lax.Precision.HIGHEST, preferred_element_t...  65.2 us
    scatter x16, other arithmetic, visit(): return (grads.at[index].set(g_win), probe_grads.at[index].set(g_probe))  44.5 us
    another operation x1, loops' own time, process(): return lax.fori_loop(0, count, visit, init)  25.7 us
    scatter-add x6, other arithmetic, on_device(): grad_pad = grad_pad.at[:, :, row * step:row * step + size, col * step:col...  16.2 us
    another operation x23, other arithmetic  16 us
  transfers between devices with their start and end apart: 5, of which 5 were waited for; matrix products, arithmetic and copies ran while one was open for 2% of the time, Pallas kernels for 0%

commit v1 on v0

v1 whole, which is shorter than its diff:
```python
import functools

import jax
import jax.numpy as jnp
import ml_dtypes
import numpy as np
from jax import lax
from jax.experimental import pallas as pl
from jax.experimental.pallas import tpu as pltpu
from jax.sharding import PartitionSpec as P

SIDE, HALF = 256, 128
PHASE_SCALE = 40.0

def embed(m):
    return np.block([[m.real, m.imag], [-m.imag, m.real]])

def tables():
    n = np.arange(SIDE)
    dft = np.exp(-2j * np.pi * (n[:, None] * n[None, :] % SIDE) / SIDE) / 16.0
    signed = np.where(n < HALF, n, n - SIDE) / SIDE
    spread = np.exp(-1j * PHASE_SCALE * signed**2)
    move = np.conj(dft) @ (spread[:, None] * dft)
    near, across = move[:HALF, :HALF], move[:HALF, HALF:]
    ce, co = (near + across) / 2, (near - across) / 2
    a, b = dft[:HALF, 0::2], dft[:HALF, 1::2]
    right = [embed(ce), embed(co), embed(a), embed(b), embed(b.T)]
    full = np.stack(right + [m.T for m in right])
    hi = full.astype(ml_dtypes.bfloat16)
    lo = (full - hi.astype(np.float64)).astype(ml_dtypes.bfloat16)
    order = np.concatenate([np.arange(0, SIDE, 2), np.arange(1, SIDE, 2)])
    perm = np.zeros((SIDE, SIDE))
    perm[order, n] = 1.0
    return np.concatenate([hi, lo, perm[None].astype(ml_dtypes.bfloat16)])

CE, CO, FA, FB, FBT = range(5)
LEFT = 5
LOW = 10
PERM = 20

def split(x):
    hi = x.astype(jnp.bfloat16)
    return hi, (x - hi.astype(jnp.float32)).astype(jnp.bfloat16)

def dot(l, r):
    return jnp.dot(l, r, preferred_element_type=jnp.float32)

def mul_right(x, tab, k):
    hi, lo = split(x)
    wh, wl = tab[k], tab[k + LOW]
    return dot(hi, wh) + dot(lo, wh) + dot(hi, wl)

def mul_left(x, tab, k):
    hi, lo = split(x)
    wh, wl = tab[k + LEFT], tab[k + LEFT + LOW]
    return dot(wh, hi) + dot(wl, hi) + dot(wh, lo)

def lanes(re, im):
    rl, rr, il, ir = re[:, :HALF], re[:, HALF:], im[:, :HALF], im[:, HALF:]
    cat = lambda p, q: jnp.concatenate([p, q], axis=1)
    return cat(rl + rr, il + ir), cat(rl - rr, il - ir)

def rows(re, im):
    rt, rb, it, ib = re[:HALF], re[HALF:], im[:HALF], im[HALF:]
    cat = lambda p, q: jnp.concatenate([p, q], axis=0)
    return cat(rt + rb, it + ib), cat(rt - rb, it - ib)

def planes_of_lanes(even, odd):
    re = jnp.concatenate([even[:, :HALF], odd[:, :HALF]], axis=1)
    im = jnp.concatenate([even[:, HALF:], odd[:, HALF:]], axis=1)
    return re, im

def planes_of_rows(even, odd):
    re = jnp.concatenate([even[:HALF], odd[:HALF]], axis=0)
    im = jnp.concatenate([even[HALF:], odd[HALF:]], axis=0)
    return re, im

def spread(re, im, tab):
    e, o = lanes(re, im)
    e, o = mul_right(e, tab, CE), mul_right(o, tab, CO)
    yield
    re, im = planes_of_lanes(e, o)
    e, o = rows(re, im)
    e, o = mul_left(e, tab, CE), mul_left(o, tab, CO)
    yield
    re, im = planes_of_rows(e + o, e - o)
    l = lambda t: jnp.concatenate([t[:, :HALF] + t[:, HALF:], t[:, :HALF] - t[:, HALF:]], axis=1)
    return l(re), l(im)

def to_far(re, im, tab):
    e, o = lanes(re, im)
    e, o = mul_right(e, tab, FA), mul_right(o, tab, FB)
    yield
    re, im = planes_of_lanes(e, o)
    e, o = rows(re, im)
    e, o = mul_left(e, tab, FA), mul_left(o, tab, FB)
    yield
    return e, o

def from_far(even, odd, tab):
    e, o = mul_left(even, tab, FA), mul_left(odd, tab, FBT)
    yield
    re, im = planes_of_rows(e + o, e - o)
    e = jnp.concatenate([re[:, :HALF], im[:, :HALF]], axis=1)
    o = jnp.concatenate([re[:, HALF:], im[:, HALF:]], axis=1)
    e, o = mul_right(e, tab, FA), mul_right(o, tab, FBT)
    yield
    return planes_of_lanes(e + o, e - o)

def point(weight, pad, grad, meas, probe, pgrad, tab, order, a, b):
    r = pl.ds(pl.multiple_of(a * HALF, HALF), SIDE)
    c = pl.ds(pl.multiple_of(b * HALF, HALF), SIDE)
    pr, pi = probe[0], probe[1]
    o0r, o0i = pad[0, 0, r, c], pad[0, 1, r, c]
    ur, ui = yield from spread(pr * o0r - pi * o0i, pr * o0i + pi * o0r, tab)
    o1r, o1i = pad[1, 0, r, c], pad[1, 1, r, c]
    even, odd = yield from to_far(ur * o1r - ui * o1i, ur * o1i + ui * o1r, tab)
    hi, lo = split(meas[a, b])
    m = dot(hi, tab[PERM]) + dot(lo, tab[PERM])
    order[0], order[1] = m[:, :HALF], m[:, HALF:]

    def pull(f, start):
        pick = pl.ds(start, HALF, stride=2)
        m = jnp.concatenate([order[0, pick, :], order[1, pick, :]], axis=1)
        fr, fi = f[:HALF], f[HALF:]
        d = (fr * fr + fi * fi - m) * (2.0 * weight)
        return jnp.concatenate([d * fr, -(d * fi)], axis=0)

    gr, gi = yield from from_far(pull(even, 0), pull(odd, 1), tab)
    grad[1, 0, r, c] += ur * gr - ui * gi
    grad[1, 1, r, c] -= ur * gi + ui * gr
    o1r, o1i = pad[1, 0, r, c], pad[1, 1, r, c]
    gr, gi = yield from spread(o1r * gr - o1i * gi, o1r * gi + o1i * gr, tab)
    pr, pi = probe[0], probe[1]
    grad[0, 0, r, c] += pr * gr - pi * gi
    grad[0, 1, r, c] -= pr * gi + pi * gr
    o0r, o0i = pad[0, 0, r, c], pad[0, 1, r, c]
    pgrad[0:SIDE] += o0r * gr - o0i * gi
    pgrad[SIDE:] -= o0r * gi + o0i * gr


def run(work):
    work = list(work)
    while work:
        for w in list(work):
            if next(w, work) is work:
                work.remove(w)


MESH = pl.DeviceIdType.MESH


def kernel(tiles, pats, scanned, obj, meas_in, probe_in, tab_in, out_obj, out_probe,
           pad, grad, meas, probe, tab, order, pgrad, from_left, from_up, part1, part2, share, total,
           local_sem, halo_send, halo_recv, grad_send, grad_recv, sum_send, sum_recv):
    tile, pat = lax.axis_index("tile"), lax.axis_index("pat")
    left, right = {"pat": lax.rem(pat + pats - 1, pats)}, {"pat": lax.rem(pat + 1, pats)}
    up, down = {"tile": lax.rem(tile + tiles - 1, tiles)}, {"tile": lax.rem(tile + 1, tiles)}

    def remote(src, dst, send, recv, k, device):
        return pltpu.make_async_remote_copy(
            src_ref=src, dst_ref=dst, send_sem=send.at[k], recv_sem=recv.at[k],
            device_id=device, device_id_type=MESH)

    loads = [
        pltpu.make_async_copy(obj, pad.at[:, :, pl.ds(0, 512), pl.ds(0, 256)], local_sem.at[0]),
        pltpu.make_async_copy(probe_in, probe, local_sem.at[1]),
        pltpu.make_async_copy(tab_in, tab, local_sem.at[2]),
        pltpu.make_async_copy(meas_in, meas, local_sem.at[3]),
    ]
    for copy in loads:
        copy.start()

    barrier = pltpu.get_barrier_semaphore()
    for o in range(1, tiles):
        pl.semaphore_signal(barrier, inc=1, device_id={"tile": lax.rem(tile + o, tiles)}, device_id_type=MESH)
    for o in range(1, pats):
        pl.semaphore_signal(barrier, inc=1, device_id={"pat": lax.rem(pat + o, pats)}, device_id_type=MESH)
    grad[...] = jnp.zeros_like(grad)
    pgrad[...] = jnp.zeros_like(pgrad)
    pl.semaphore_wait(barrier, tiles - 1 + pats - 1)

    first, second = pl.ds(0, HALF), pl.ds(256, HALF)
    chunk = [pl.ds(k * HALF, HALF) for k in range(5)]
    beside = [
        remote(obj.at[:, :, chunk[k], first], pad.at[:, :, chunk[k], second], halo_send, halo_recv, k, left)
        for k in range(4)
    ]
    below = remote(obj.at[:, :, chunk[0], :], pad.at[:, :, chunk[4], pl.ds(0, 256)], halo_send, halo_recv, 4, up)
    corner = remote(pad.at[:, :, chunk[0], second], pad.at[:, :, chunk[4], second], halo_send, halo_recv, 5, up)
    for k in (3, 0, 1, 2):
        beside[k].start()
    below.start()
    for copy in loads:
        copy.wait()

    low = remote(grad.at[:, :, chunk[4], :], from_up, grad_send, grad_recv, 4, down)
    out = [
        remote(grad.at[:, :, chunk[k], second], from_left.at[:, :, chunk[k], :], grad_send, grad_recv, k, right)
        for k in range(4)
    ]

    def step(i, _):
        @pl.when(i == 1)
        def _():
            below.wait()

        @pl.when(i == 2)
        def _():
            beside[3].wait()
            beside[0].wait()
            corner.start()
            beside[1].wait()
            corner.wait()

        @pl.when(i == 3)
        def _():
            low.start()
            beside[2].wait()

        ahead = i < 2
        b = i // 2
        a0 = jnp.where(ahead, 2 * i, 7 - 2 * i)
        a1 = jnp.where(ahead, 2 * i + 1, 2 * i - 4)
        run(
            point(scanned[a, b].astype(jnp.float32), pad, grad, meas, probe, pgrad, tab, order.at[k], a, b)
            for k, a in enumerate((a0, a1))
        )
        return 0

    lax.fori_loop(0, 4, step, 0)

    rows_of = lambda t: pl.ds(pl.multiple_of(t * 64, 64), 64)
    cell = lambda p: (pl.ds(pl.multiple_of((p // 2) * 8, 8), 8), pl.ds(pl.multiple_of((p % 2) * HALF, HALF), HALF))
    flat = pgrad
    sums1, sums2, spread2, spread1 = [], [], [], []
    for o in range(1, tiles):
        t = lax.rem(tile + o, tiles)
        sums1.append(remote(flat.at[rows_of(t), :], part1.at[o - 1], sum_send, sum_recv, o - 1, {"tile": t}))
    for copy in sums1:
        copy.start()

    for k in (1, 2, 3):
        out[k].start()
    low.wait()
    grad[:, :, 0:HALF, :] += from_up[...]
    out[0].start()

    for copy in sums1:
        copy.wait()
    acc = flat[rows_of(tile), :]
    for k in range(tiles - 1):
        acc = acc + part1[k]
    share[...] = acc
    for o in range(1, pats):
        p = lax.rem(pat + o, pats)
        sums2.append(remote(share.at[cell(p)], part2.at[o - 1], sum_send, sum_recv, 7 + o - 1, {"pat": p}))
    for copy in sums2:
        copy.start()
    for copy in sums2:
        copy.wait()
    acc = share[cell(pat)]
    for k in range(pats - 1):
        acc = acc + part2[k]
    mine = total.at[rows_of(tile), :]
    total_cell = mine.at[cell(pat)]
    total_cell[...] = acc
    for o in range(1, pats):
        p = lax.rem(pat + o, pats)
        spread2.append(remote(total_cell, total_cell, sum_send, sum_recv, 22 + o - 1, {"pat": p}))
    for copy in spread2:
        copy.start()
    for copy in spread2:
        copy.wait()
    for o in range(1, tiles):
        t = lax.rem(tile + o, tiles)
        spread1.append(remote(mine, mine, sum_send, sum_recv, 37 + o - 1, {"tile": t}))
    for copy in spread1:
        copy.start()

    stores = []
    for n, k in enumerate((1, 2, 3, 0)):
        out[k].wait()
        grad[:, :, chunk[k], 0:HALF] += from_left[:, :, chunk[k], :]
        store = pltpu.make_async_copy(
            grad.at[:, :, chunk[k], pl.ds(0, 256)], out_obj.at[:, :, chunk[k], :], local_sem.at[4 + n])
        store.start()
        stores.append(store)
    for copy in spread1:
        copy.wait()
    last = pltpu.make_async_copy(total, out_probe, local_sem.at[8])
    last.start()
    for copy in stores:
        copy.wait()
    last.wait()


def on_device(scanned, measured, obj, probe):
    tiles, pats = lax.axis_size("tile"), lax.axis_size("pat")
    table = jnp.asarray(tables())
    anywhere = pl.BlockSpec(memory_space=pl.ANY)
    f32 = jnp.float32
    vmem = lambda *shape: pltpu.VMEM(shape, f32)
    dma = lambda n: pltpu.SemaphoreType.DMA((n,))
    sums = 2 * (tiles - 1 + pats - 1)
    grad_obj, grad_probe = pl.pallas_call(
        functools.partial(kernel, tiles, pats),
        out_shape=[jax.ShapeDtypeStruct(obj.shape, f32), jax.ShapeDtypeStruct((2 * SIDE, SIDE), f32)],
        in_specs=[pl.BlockSpec(memory_space=pltpu.SMEM)] + [anywhere] * 4,
        out_specs=[anywhere, anywhere],
        scratch_shapes=[
            vmem(2, 2, 640, 384), vmem(2, 2, 640, 384), vmem(4, 2, SIDE, SIDE), vmem(2, SIDE, SIDE),
            pltpu.VMEM(table.shape, jnp.bfloat16), vmem(2, 2, SIDE, HALF), vmem(2 * SIDE, SIDE),
            vmem(2, 2, 512, HALF), vmem(2, 2, HALF, 384),
            vmem(tiles - 1, 64, SIDE), vmem(pats - 1, 8, HALF), vmem(64, SIDE), vmem(2 * SIDE, SIDE),
            dma(9), dma(6), dma(6), dma(5), dma(5), dma(sums), dma(sums),
        ],
        compiler_params=pltpu.CompilerParams(
            collective_id=0, has_side_effects=True, vmem_limit_bytes=56 * 2**20),
        cost_estimate=pl.CostEstimate(flops=27 * 10**9, bytes_accessed=10 * 2**20, transcendentals=0),
    )(scanned, obj, measured, probe, table)
    return grad_obj, grad_probe.reshape(probe.shape)


def solution(mesh):
    in_specs = (P("tile", "pat"), P("tile", "pat", None, None), P(None, None, "tile", "pat"), P())
    out_specs = (P(None, None, "tile", "pat"), P())
    return jax.shard_map(
        on_device, mesh=mesh, in_specs=in_specs, out_specs=out_specs, check_vma=False
    )
```

time: 682 us -> 86.8 us (0.13)
  waiting for transfers between devices: 226 us -> 0 us
  starting transfers between devices: 202 us -> 0 us
  other arithmetic: 87.8 us -> 0 us
  Pallas kernels: 0 us -> 80.7 us
  matrix products: 65.2 us -> 0 us
  local copies, waits for them, and re-layouts: 54 us -> 5.24 us
  loops' own time: 26.7 us -> 0 us
  between operations: 14.6 us -> 0.65 us
    ppermute x4 -> x0, starting transfers between devices: 202 us -> none  [passed_along(): return lax.ppermute(block, axis, route)]
    psum x1 -> x0, waiting for transfers between devices: 148 us -> none  [on_device(): grad_probe = lax.psum(probe_local, ('pat', 'tile'))]
    pallas_call x0 -> x1, Pallas kernels: none -> 80.7 us  [on_device(): pl.pallas_call(functools.partial(kernel, tiles, pats), out_shape=[jax.Sha...]
    ppermute x4 -> x0, waiting for transfers between devices: 78.3 us -> none  [passed_along(): return lax.ppermute(block, axis, route)]
    dot_general x96 -> x0, matrix products: 65.2 us -> none  [matmul(): jnp.dot(left, right, precision=lax.Precision.HIGHEST, preferred_element_t...]
    scatter x16 -> x0, other arithmetic: 44.5 us -> none  [visit(): return (grads.at[index].set(g_win), probe_grads.at[index].set(g_probe))]
    another operation x9 -> x0, loops' own time: 26.7 us -> none  [the longest x1 25.7 us: process(): return lax.fori_loop(0, count, visit, init)]
    scatter-add x8 -> x0, other arithmetic: 18.8 us -> none  [the longest x6 16.2 us: on_device(): grad_pad = grad_pad.at[:, :, row * step:row * step + size, col * step:col...]
  transfers between devices with their start and end apart: 5 -> 0, of which waited for: 5 -> 0; matrix products, arithmetic and copies ran while one was open for 2% -> 0% of each run, Pallas kernels for 0% -> 0%
where the time goes in v1:
time: 86.8 us; the launch traced here: 86.6 us
  Pallas kernels  80.7 us (93%)
  local copies, waits for them, and re-layouts  5.24 us (6%)
    pallas_call x1, Pallas kernels, on_device(): pl.pallas_call(functools.partial(kernel, tiles, pats), out_shape=[jax.Sha...  80.7 us
    unnamed x5, local copies, waits for them, and re-layouts  5.24 us

profile of v1, /device:TPU:1, one launch (start us, length us, event | category | flops | bytes accessed | tf_op | source)
XLA Modules:
  0.0 86.6 jit_solution(1970064427267342582)
XLA Ops:
  0.6 1.3 %copy.7.scanned = s32[4,2]{1,0:T(4,128)} copy(s32[4,2]{0,1:T(2,128)} %param.5) | data formatting | bytes 64 | tf_op args[0]
  2.0 80.7 %shard_map.68 = (f32[2,2,512,256]{3,2,1,0:T(8,128)}, f32[512,256]{1,0:T(8,128)}) custom-call(s32[4,2]{1,0:T(4,128)} %copy.7.scanned, f32[2,2,512,256]{3,2,1,0:T(8,128)} %obj.1, f32[4,2,256,256]{3,2,1,0:T(8,128)} %meas_in.1, f32[2,256,256]{2,1,0:T(8,128)} %probe_in.1, bf16[21,256,256]{2,1,0:T(8,128)(2,1)} %constant.2.clone.tab_in), custom_call_target="tpu_custom_call" | custom-call | flops 27000000512 | bytes 10485760 | tf_op jit(solution)/shard_map/pallas_call | solution.py:306
  82.7 0.0 copy-start
  82.7 3.1 %copy.10 = f32[2,2,512,256]{3,2,1,0:T(8,128)} copy(f32[2,2,512,256]{3,2,1,0:T(8,128)} %get-tuple-element.8) | data formatting | bytes 4194304
  85.8 0.0 copy-done
  85.8 0.8 copy.11
Async XLA Ops:
  82.7 3.1 %copy-start = (f32[512,256]{1,0:T(8,128)S(1)}, f32[512,256]{1,0:T(8,128)}, u32[]{:S(2)}) copy-start(f32[512,256]{1,0:T(8,128)} %get-tuple-element.5) | copy-start | bytes 1572868

commit v2 on v1

--- a/solution.py
+++ b/solution.py
@@ -107,9 +107,12 @@
     yield
     return planes_of_lanes(e + o, e - o)
 
-def point(weight, pad, grad, meas, probe, pgrad, tab, order, a, b):
+def point(scanned, pad, grad, meas, probe, pgrad, tab, order, a, b):
     r = pl.ds(pl.multiple_of(a * HALF, HALF), SIDE)
     c = pl.ds(pl.multiple_of(b * HALF, HALF), SIDE)
+    here = [lax.broadcasted_iota(jnp.int32, scanned.shape, n) == v for n, v in enumerate((a, b))]
+    live = jnp.where(here[0] & here[1], scanned[...].astype(jnp.float32), 0.0)
+    weight = jnp.sum(jnp.sum(live, axis=1, keepdims=True), axis=0, keepdims=True)
     pr, pi = probe[0], probe[1]
     o0r, o0i = pad[0, 0, r, c], pad[0, 1, r, c]
     ur, ui = yield from spread(pr * o0r - pi * o0i, pr * o0i + pi * o0r, tab)
@@ -150,9 +153,9 @@
 MESH = pl.DeviceIdType.MESH
 
 
-def kernel(tiles, pats, scanned, obj, meas_in, probe_in, tab_in, out_obj, out_probe,
-           pad, grad, meas, probe, tab, order, pgrad, from_left, from_up, part1, part2, share, total,
-           local_sem, halo_send, halo_recv, grad_send, grad_recv, sum_send, sum_recv):
+def kernel(tiles, pats, scanned_in, obj, meas_in, probe_in, tab_in, out_obj, out_probe,
+           scanned, pad, grad, meas, probe, tab, order, pgrad, from_left, from_up, half, part, total,
+           local_sem, halo_send, halo_recv, grad_send, grad_recv, sum_send, sum_recv, inside):
     tile, pat = lax.axis_index("tile"), lax.axis_index("pat")
     left, right = {"pat": lax.rem(pat + pats - 1, pats)}, {"pat": lax.rem(pat + 1, pats)}
     up, down = {"tile": lax.rem(tile + tiles - 1, tiles)}, {"tile": lax.rem(tile + 1, tiles)}
@@ -167,6 +170,7 @@
         pltpu.make_async_copy(probe_in, probe, local_sem.at[1]),
         pltpu.make_async_copy(tab_in, tab, local_sem.at[2]),
         pltpu.make_async_copy(meas_in, meas, local_sem.at[3]),
+        pltpu.make_async_copy(scanned_in, scanned, local_sem.at[9]),
     ]
     for copy in loads:
         copy.start()
@@ -182,24 +186,39 @@
 
     first, second = pl.ds(0, HALF), pl.ds(256, HALF)
     chunk = [pl.ds(k * HALF, HALF) for k in range(5)]
+    piece = [pl.ds(k * 64, 64) for k in range(8)]
     beside = [
-        remote(obj.at[:, :, chunk[k], first], pad.at[:, :, chunk[k], second], halo_send, halo_recv, k, left)
-        for k in range(4)
+        remote(obj.at[:, :, piece[k], first], pad.at[:, :, piece[k], second], halo_send, halo_recv, k, left)
+        for k in range(8)
     ]
-    below = remote(obj.at[:, :, chunk[0], :], pad.at[:, :, chunk[4], pl.ds(0, 256)], halo_send, halo_recv, 4, up)
-    corner = remote(pad.at[:, :, chunk[0], second], pad.at[:, :, chunk[4], second], halo_send, halo_recv, 5, up)
-    for k in (3, 0, 1, 2):
-        beside[k].start()
+    below = remote(obj.at[:, :, chunk[0], :], pad.at[:, :, chunk[4], pl.ds(0, 256)], halo_send, halo_recv, 8, up)
+    corner = remote(pad.at[:, :, chunk[0], second], pad.at[:, :, chunk[4], second], halo_send, halo_recv, 9, up)
+    core = lax.rem(tile, 2)
+
+    @pl.when(core == 0)
+    def _():
+        for k in range(8):
+            beside[k].start()
+
     below.start()
     for copy in loads:
         copy.wait()
 
-    low = remote(grad.at[:, :, chunk[4], :], from_up, grad_send, grad_recv, 4, down)
+    low_first = remote(
+        grad.at[:, :, chunk[4], first], from_up.at[:, :, :, first], grad_send, grad_recv, 6, down)
+    low = remote(
+        grad.at[:, :, chunk[4], chunk[1]], from_up.at[:, :, :, chunk[1]], grad_send, grad_recv, 4, down)
+    low_corner = remote(
+        grad.at[:, :, chunk[4], second], from_up.at[:, :, :, second], grad_send, grad_recv, 5, down)
     out = [
         remote(grad.at[:, :, chunk[k], second], from_left.at[:, :, chunk[k], :], grad_send, grad_recv, k, right)
         for k in range(4)
     ]
 
+    def add_corner():
+        grad[:, :, 0:HALF, 256:] += from_up[:, :, :, 256:]
+        out[0].start()
+
     def step(i, _):
         @pl.when(i == 1)
         def _():
@@ -207,87 +226,120 @@
 
         @pl.when(i == 2)
         def _():
-            beside[3].wait()
-            beside[0].wait()
-            corner.start()
-            beside[1].wait()
-            corner.wait()
+            @pl.when(core == 1)
+            def _():
+                for k in range(3):
+                    beside[k].start()
+
+            for o in range(1, pats):
+                pl.semaphore_signal(inside, inc=1, device_id={"pat": lax.rem(pat + o, pats)}, device_id_type=MESH)
+            low_first.start()
+            for k in range(5):
+                beside[k].wait_send()
+                pl.when(core == 1)(beside[k + 3].start)
+                if k == 2:
+                    beside[0].wait_recv()
+                    beside[1].wait_recv()
+                    corner.start()
+            for k in range(2, 6):
+                beside[k].wait_recv()
 
         @pl.when(i == 3)
         def _():
-            low.start()
-            beside[2].wait()
-
-        ahead = i < 2
+            out[1].start()
+
+            @pl.when(core == 1)
+            def _():
+                low_corner.wait_recv()
+                add_corner()
+
+            for k in range(5, 8):
+                beside[k].wait_send()
+            beside[6].wait_recv()
+            beside[7].wait_recv()
+            corner.wait()
+
         b = i // 2
-        a0 = jnp.where(ahead, 2 * i, 7 - 2 * i)
-        a1 = jnp.where(ahead, 2 * i + 1, 2 * i - 4)
+        a = 2 * i - 4 * b
         run(
-            point(scanned[a, b].astype(jnp.float32), pad, grad, meas, probe, pgrad, tab, order.at[k], a, b)
-            for k, a in enumerate((a0, a1))
+            point(scanned, pad, grad, meas, probe, pgrad, tab, order.at[k], a + k, b)
+            for k in range(2)
         )
         return 0
 
     lax.fori_loop(0, 4, step, 0)
 
-    rows_of = lambda t: pl.ds(pl.multiple_of(t * 64, 64), 64)
-    cell = lambda p: (pl.ds(pl.multiple_of((p // 2) * 8, 8), 8), pl.ds(pl.multiple_of((p % 2) * HALF, HALF), HALF))
-    flat = pgrad
-    sums1, sums2, spread2, spread1 = [], [], [], []
-    for o in range(1, tiles):
-        t = lax.rem(tile + o, tiles)
-        sums1.append(remote(flat.at[rows_of(t), :], part1.at[o - 1], sum_send, sum_recv, o - 1, {"tile": t}))
-    for copy in sums1:
-        copy.start()
-
-    for k in (1, 2, 3):
-        out[k].start()
-    low.wait()
-    grad[:, :, 0:HALF, :] += from_up[...]
-    out[0].start()
-
-    for copy in sums1:
-        copy.wait()
-    acc = flat[rows_of(tile), :]
-    for k in range(tiles - 1):
-        acc = acc + part1[k]
-    share[...] = acc
-    for o in range(1, pats):
-        p = lax.rem(pat + o, pats)
-        sums2.append(remote(share.at[cell(p)], part2.at[o - 1], sum_send, sum_recv, 7 + o - 1, {"pat": p}))
-    for copy in sums2:
-        copy.start()
-    for copy in sums2:
-        copy.wait()
-    acc = share[cell(pat)]
-    for k in range(pats - 1):
-        acc = acc + part2[k]
-    mine = total.at[rows_of(tile), :]
-    total_cell = mine.at[cell(pat)]
-    total_cell[...] = acc
-    for o in range(1, pats):
-        p = lax.rem(pat + o, pats)
-        spread2.append(remote(total_cell, total_cell, sum_send, sum_recv, 22 + o - 1, {"pat": p}))
-    for copy in spread2:
-        copy.start()
-    for copy in spread2:
-        copy.wait()
-    for o in range(1, tiles):
-        t = lax.rem(tile + o, tiles)
-        spread1.append(remote(mine, mine, sum_send, sum_recv, 37 + o - 1, {"tile": t}))
-    for copy in spread1:
-        copy.start()
+    other = {"tile": tile + 1 - 2 * core}
+    layer, side_x, side_y = tile // 2, pat // 4, lax.rem(pat, 4)
+    half_of = lambda c: pl.ds(pl.multiple_of(c * 256, 256), 256)
+    trips = [(x, y, z) for x in range(4) for y in range(4) for z in range(4)][1:]
+    trips.sort(key=lambda t: -sum(min(n, 4 - n) for n in t))
+
+    def goal(trip):
+        x, y, z = (lax.rem(v + n, 4) for v, n in zip((side_x, side_y, layer), trip))
+        return (x * 4 + y) * 4 + z, {"pat": x * 4 + y, "tile": z * 2 + core}
+
+    def cell(c):
+        return (pl.ds(pl.multiple_of(core * 256 + (c // 2) * 8, 8), 8),
+                pl.ds(pl.multiple_of(lax.rem(c, 2) * HALF, HALF), HALF))
+
+    own = cell(goal((0, 0, 0))[0])
+    swap = remote(pgrad.at[half_of(1 - core), :], half, sum_send, sum_recv, 0, other)
+    swap.start()
+    low_corner.start()
+
+    @pl.when(core == 0)
+    def _():
+        out[2].start()
+        out[3].start()
+
+    pl.semaphore_wait(inside, pats - 1)
+    swap.wait()
+    pgrad[half_of(core), :] += half[...]
+    for n, trip in enumerate(trips):
+        c, device = goal(trip)
+        remote(pgrad.at[cell(c)], part.at[n], sum_send, sum_recv, 1, device).start()
+    low_corner.wait_send()
+    low.start()
+    pl.when(core == 1)(out[2].start)
+    remote(part, part, sum_send, sum_recv, 1, other).wait()
+    acc = pgrad[own]
+    for n in range(len(trips)):
+        acc = acc + part[n]
+    total[own] = acc
+    for trip in trips:
+        remote(total.at[own], total.at[own], sum_send, sum_recv, 2, goal(trip)[1]).start()
+
+    pl.when(core == 1)(out[3].start)
+
+    @pl.when(core == 0)
+    def _():
+        low_corner.wait_recv()
+        add_corner()
 
     stores = []
-    for n, k in enumerate((1, 2, 3, 0)):
+
+    def finish(k):
         out[k].wait()
+        if k == 0:
+            low_first.wait()
+            low.wait()
+            grad[:, :, 0:HALF, 0:256] += from_up[:, :, :, 0:256]
         grad[:, :, chunk[k], 0:HALF] += from_left[:, :, chunk[k], :]
         store = pltpu.make_async_copy(
-            grad.at[:, :, chunk[k], pl.ds(0, 256)], out_obj.at[:, :, chunk[k], :], local_sem.at[4 + n])
+            grad.at[:, :, chunk[k], pl.ds(0, 256)], out_obj.at[:, :, chunk[k], :], local_sem.at[4 + k])
         store.start()
         stores.append(store)
-    for copy in spread1:
-        copy.wait()
+
+    finish(1)
+    remote(part, part, sum_send, sum_recv, 2, other).wait()
+    mine = total.at[half_of(core), :]
+    back = remote(mine, mine, sum_send, sum_recv, 3, other)
+    back.start()
+    finish(2)
+    finish(3)
+    finish(0)
+    back.wait()
     last = pltpu.make_async_copy(total, out_probe, local_sem.at[8])
     last.start()
     for copy in stores:
@@ -302,18 +354,17 @@
     f32 = jnp.float32
     vmem = lambda *shape: pltpu.VMEM(shape, f32)
     dma = lambda n: pltpu.SemaphoreType.DMA((n,))
-    sums = 2 * (tiles - 1 + pats - 1)
     grad_obj, grad_probe = pl.pallas_call(
         functools.partial(kernel, tiles, pats),
         out_shape=[jax.ShapeDtypeStruct(obj.shape, f32), jax.ShapeDtypeStruct((2 * SIDE, SIDE), f32)],
-        in_specs=[pl.BlockSpec(memory_space=pltpu.SMEM)] + [anywhere] * 4,
+        in_specs=[anywhere] * 5,
         out_specs=[anywhere, anywhere],
         scratch_shapes=[
-            vmem(2, 2, 640, 384), vmem(2, 2, 640, 384), vmem(4, 2, SIDE, SIDE), vmem(2, SIDE, SIDE),
+            pltpu.VMEM(scanned.shape, jnp.int32), vmem(2, 2, 640, 384), vmem(2, 2, 640, 384), vmem(4, 2, SIDE, SIDE), vmem(2, SIDE, SIDE),
             pltpu.VMEM(table.shape, jnp.bfloat16), vmem(2, 2, SIDE, HALF), vmem(2 * SIDE, SIDE),
             vmem(2, 2, 512, HALF), vmem(2, 2, HALF, 384),
-            vmem(tiles - 1, 64, SIDE), vmem(pats - 1, 8, HALF), vmem(64, SIDE), vmem(2 * SIDE, SIDE),
-            dma(9), dma(6), dma(6), dma(5), dma(5), dma(sums), dma(sums),
+            vmem(SIDE, SIDE), vmem(63, 8, HALF), vmem(2 * SIDE, SIDE),
+            dma(10), dma(10), dma(10), dma(7), dma(7), dma(4), dma(4), pltpu.SemaphoreType.REGULAR,
         ],
         compiler_params=pltpu.CompilerParams(
             collective_id=0, has_side_effects=True, vmem_limit_bytes=56 * 2**20),

time: 86.8 us -> 71.6 us (0.82)
  Pallas kernels: 80.7 us -> 65.5 us
    pallas_call x1, Pallas kernels: 80.7 us -> 65.5 us  [on_device(): pl.pallas_call(functools.partial(kernel, tiles, pats), out_shape=[jax.Sha...]
where the time goes in v2:
time: 71.6 us; the launch traced here: 71.4 us
  Pallas kernels  65.5 us (91%)
  local copies, waits for them, and re-layouts  5.24 us (7%)
    pallas_call x1, Pallas kernels, on_device(): pl.pallas_call(functools.partial(kernel, tiles, pats), out_shape=[jax.Sha...  65.5 us
    unnamed x5, local copies, waits for them, and re-layouts  5.24 us

profile of v2, /device:TPU:1, one launch (start us, length us, event | category | flops | bytes accessed | tf_op | source)
XLA Modules:
  0.0 71.4 jit_solution(5848718111592177910)
XLA Ops:
  0.6 1.3 %copy.7.scanned_in = s32[4,2]{1,0:T(4,128)} copy(s32[4,2]{0,1:T(2,128)} %param.5) | data formatting | bytes 64 | tf_op args[0]
  2.0 65.5 %shard_map.68 = (f32[2,2,512,256]{3,2,1,0:T(8,128)}, f32[512,256]{1,0:T(8,128)}) custom-call(s32[4,2]{1,0:T(4,128)} %copy.7.scanned_in, f32[2,2,512,256]{3,2,1,0:T(8,128)} %obj.1, f32[4,2,256,256]{3,2,1,0:T(8,128)} %meas_in.1, f32[2,256,256]{2,1,0:T(8,128)} %probe_in.1, bf16[21,256,256]{2,1,0:T(8,128)(2,1)} %constant.2.clone.tab_in), custom_call_target="tpu_custom_call" | custom-call | flops 27000000512 | bytes 10485760 | tf_op jit(solution)/shard_map/pallas_call | solution.py:357
  67.5 0.0 copy-start
  67.5 3.1 %copy.10 = f32[2,2,512,256]{3,2,1,0:T(8,128)} copy(f32[2,2,512,256]{3,2,1,0:T(8,128)} %get-tuple-element.8) | data formatting | bytes 4194304
  70.6 0.0 copy-done
  70.6 0.8 %copy.11 = f32[2,256,256]{2,1,0:T(8,128)} copy(f32[2,256,256]{2,1,0:T(8,128)S(1)} %bitcast.1) | data formatting | bytes 1048576
Async XLA Ops:
  67.5 3.1 %copy-start = (f32[512,256]{1,0:T(8,128)S(1)}, f32[512,256]{1,0:T(8,128)}, u32[]{:S(2)}) copy-start(f32[512,256]{1,0:T(8,128)} %get-tuple-element.5) | copy-start | bytes 1572868

commit v3 on v2

--- a/solution.py
+++ b/solution.py
@@ -110,7 +110,7 @@
 def point(scanned, pad, grad, meas, probe, pgrad, tab, order, a, b):
     r = pl.ds(pl.multiple_of(a * HALF, HALF), SIDE)
     c = pl.ds(pl.multiple_of(b * HALF, HALF), SIDE)
-    here = [lax.broadcasted_iota(jnp.int32, scanned.shape, n) == v for n, v in enumerate((a, b))]
+    here = [lax.broadcasted_iota(jnp.int32, scanned.shape, n) == v for n, v in enumerate((b, a))]
     live = jnp.where(here[0] & here[1], scanned[...].astype(jnp.float32), 0.0)
     weight = jnp.sum(jnp.sum(live, axis=1, keepdims=True), axis=0, keepdims=True)
     pr, pi = probe[0], probe[1]
@@ -317,34 +317,25 @@
         low_corner.wait_recv()
         add_corner()
 
-    stores = []
-
     def finish(k):
         out[k].wait()
         if k == 0:
             low_first.wait()
             low.wait()
             grad[:, :, 0:HALF, 0:256] += from_up[:, :, :, 0:256]
-        grad[:, :, chunk[k], 0:HALF] += from_left[:, :, chunk[k], :]
-        store = pltpu.make_async_copy(
-            grad.at[:, :, chunk[k], pl.ds(0, 256)], out_obj.at[:, :, chunk[k], :], local_sem.at[4 + k])
-        store.start()
-        stores.append(store)
+        out_obj[:, :, chunk[k], 0:HALF] = grad[:, :, chunk[k], 0:HALF] + from_left[:, :, chunk[k], :]
+        out_obj[:, :, chunk[k], HALF:] = grad[:, :, chunk[k], HALF:256]
 
     finish(1)
     remote(part, part, sum_send, sum_recv, 2, other).wait()
-    mine = total.at[half_of(core), :]
-    back = remote(mine, mine, sum_send, sum_recv, 3, other)
+    mine = half_of(core)
+    back = remote(total.at[mine, :], out_probe.at[core], sum_send, sum_recv, 3, other)
     back.start()
+    out_probe[core] = total[mine, :]
     finish(2)
     finish(3)
     finish(0)
     back.wait()
-    last = pltpu.make_async_copy(total, out_probe, local_sem.at[8])
-    last.start()
-    for copy in stores:
-        copy.wait()
-    last.wait()
 
 
 def on_device(scanned, measured, obj, probe):
@@ -356,11 +347,11 @@
     dma = lambda n: pltpu.SemaphoreType.DMA((n,))
     grad_obj, grad_probe = pl.pallas_call(
         functools.partial(kernel, tiles, pats),
-        out_shape=[jax.ShapeDtypeStruct(obj.shape, f32), jax.ShapeDtypeStruct((2 * SIDE, SIDE), f32)],
+        out_shape=[pltpu.VMEM(obj.shape, f32), pltpu.VMEM(probe.shape, f32)],
         in_specs=[anywhere] * 5,
-        out_specs=[anywhere, anywhere],
+        out_specs=[pl.BlockSpec(memory_space=pltpu.VMEM)] * 2,
         scratch_shapes=[
-            pltpu.VMEM(scanned.shape, jnp.int32), vmem(2, 2, 640, 384), vmem(2, 2, 640, 384), vmem(4, 2, SIDE, SIDE), vmem(2, SIDE, SIDE),
+            pltpu.VMEM(scanned.T.shape, jnp.int32), vmem(2, 2, 640, 384), vmem(2, 2, 640, 384), vmem(4, 2, SIDE, SIDE), vmem(2, SIDE, SIDE),
             pltpu.VMEM(table.shape, jnp.bfloat16), vmem(2, 2, SIDE, HALF), vmem(2 * SIDE, SIDE),
             vmem(2, 2, 512, HALF), vmem(2, 2, HALF, 384),
             vmem(SIDE, SIDE), vmem(63, 8, HALF), vmem(2 * SIDE, SIDE),
@@ -369,8 +360,8 @@
         compiler_params=pltpu.CompilerParams(
             collective_id=0, has_side_effects=True, vmem_limit_bytes=56 * 2**20),
         cost_estimate=pl.CostEstimate(flops=27 * 10**9, bytes_accessed=10 * 2**20, transcendentals=0),
-    )(scanned, obj, measured, probe, table)
-    return grad_obj, grad_probe.reshape(probe.shape)
+    )(scanned.T, obj, measured, probe, table)
+    return grad_obj, grad_probe
 
 
 def solution(mesh):

time: 71.6 us -> 67.6 us (0.944)
  local copies, waits for them, and re-layouts: 5.24 us -> 2.11 us
    unnamed x5 -> x2, local copies, waits for them, and re-layouts: 5.24 us -> 2.11 us
    pallas_call x1, Pallas kernels: 65.5 us -> 64.8 us  [on_device(): pl.pallas_call(functools.partial(kernel, tiles, pats), out_shape=[pltpu.V...]
where the time goes in v3:
time: 67.6 us; the launch traced here: 67.5 us
  Pallas kernels  64.8 us (96%)
  local copies, waits for them, and re-layouts  2.11 us (3%)
    pallas_call x1, Pallas kernels, on_device(): pl.pallas_call(functools.partial(kernel, tiles, pats), out_shape=[pltpu.V...  64.8 us
    unnamed x2, local copies, waits for them, and re-layouts  2.11 us

profile of v3, /device:TPU:1, one launch (start us, length us, event | category | flops | bytes accessed | tf_op | source)
XLA Modules:
  0.0 67.5 jit_solution(10061724141895239074)
XLA Ops:
  0.6 64.8 %shard_map.68 = (f32[2,2,512,256]{3,2,1,0:T(8,128)S(1)}, f32[2,256,256]{2,1,0:T(8,128)S(1)}) custom-call(s32[2,4]{1,0:T(2,128)} %bitcast.1, f32[2,2,512,256]{3,2,1,0:T(8,128)} %obj.1, f32[4,2,256,256]{3,2,1,0:T(8,128)} %meas_in.1, f32[2,256,256]{2,1,0:T(8,128)} %probe_in.1, bf16[21,256,256]{2,1,0:T(8,128)(2,1)} %constant.2.clone.tab_in), custom_call_target="tpu_custom_call" | custom-call | flops 27000000512 | bytes 10485760 | tf_op jit(solution)/shard_map/pallas_call | solution.py:348
  65.4 1.3 %copy.9 = f32[2,2,512,256]{3,2,1,0:T(8,128)} copy(f32[2,2,512,256]{3,2,1,0:T(8,128)S(1)} %get-tuple-element.2) | data formatting | bytes 4194304
  66.7 0.8 %copy.10 = f32[2,256,256]{2,1,0:T(8,128)} copy(f32[2,256,256]{2,1,0:T(8,128)S(1)} %get-tuple-element.3) | data formatting | bytes 1048576

commit v4 on v3

--- a/solution.py
+++ b/solution.py
@@ -53,7 +53,8 @@
 def mul_left(x, tab, k):
     hi, lo = split(x)
     wh, wl = tab[k + LEFT], tab[k + LEFT + LOW]
-    return dot(wh, hi) + dot(wl, hi) + dot(wh, lo)
+    both = dot(jnp.concatenate([wh, wl], axis=0), hi)
+    return both[:SIDE] + both[SIDE:] + dot(wh, lo)
 
 def lanes(re, im):
     rl, rr, il, ir = re[:, :HALF], re[:, HALF:], im[:, :HALF], im[:, HALF:]
@@ -172,17 +173,14 @@
         pltpu.make_async_copy(meas_in, meas, local_sem.at[3]),
         pltpu.make_async_copy(scanned_in, scanned, local_sem.at[9]),
     ]
-    for copy in loads:
-        copy.start()
-
     barrier = pltpu.get_barrier_semaphore()
-    for o in range(1, tiles):
-        pl.semaphore_signal(barrier, inc=1, device_id={"tile": lax.rem(tile + o, tiles)}, device_id_type=MESH)
-    for o in range(1, pats):
-        pl.semaphore_signal(barrier, inc=1, device_id={"pat": lax.rem(pat + o, pats)}, device_id_type=MESH)
-    grad[...] = jnp.zeros_like(grad)
-    pgrad[...] = jnp.zeros_like(pgrad)
-    pl.semaphore_wait(barrier, tiles - 1 + pats - 1)
+    side_x, side_y = pat // 4, lax.rem(pat, 4)
+    along_x = [{"pat": lax.rem(side_x + n, 4) * 4 + side_y} for n in (1, 2, 3)]
+    along_y = [{"pat": side_x * 4 + lax.rem(side_y + n, 4)} for n in (1, 2, 3)]
+    along_tile = [{"tile": lax.rem(tile + o, tiles)} for o in (1, tiles - 1, 2, 3, 4, 5, 6)]
+    for device in [left, right] + along_y + along_x + along_tile:
+        pl.semaphore_signal(barrier, inc=1, device_id=device, device_id_type=MESH)
+    pl.semaphore_wait(barrier, tiles - 1 + 8)
 
     first, second = pl.ds(0, HALF), pl.ds(256, HALF)
     chunk = [pl.ds(k * HALF, HALF) for k in range(5)]
@@ -202,6 +200,10 @@
 
     below.start()
     for copy in loads:
+        copy.start()
+    grad[...] = jnp.zeros_like(grad)
+    pgrad[...] = jnp.zeros_like(pgrad)
+    for copy in loads:
         copy.wait()
 
     low_first = remote(
@@ -231,8 +233,8 @@
                 for k in range(3):
                     beside[k].start()
 
-            for o in range(1, pats):
-                pl.semaphore_signal(inside, inc=1, device_id={"pat": lax.rem(pat + o, pats)}, device_id_type=MESH)
+            for device in along_y:
+                pl.semaphore_signal(inside.at[0], inc=1, device_id=device, device_id_type=MESH)
             low_first.start()
             for k in range(5):
                 beside[k].wait_send()
@@ -247,6 +249,9 @@
         @pl.when(i == 3)
         def _():
             out[1].start()
+            pl.semaphore_wait(inside.at[0], 3)
+            for device in along_x:
+                pl.semaphore_signal(inside.at[1], inc=1, device_id=device, device_id_type=MESH)
 
             @pl.when(core == 1)
             def _():
@@ -270,7 +275,7 @@
     lax.fori_loop(0, 4, step, 0)
 
     other = {"tile": tile + 1 - 2 * core}
-    layer, side_x, side_y = tile // 2, pat // 4, lax.rem(pat, 4)
+    layer = tile // 2
     half_of = lambda c: pl.ds(pl.multiple_of(c * 256, 256), 256)
     trips = [(x, y, z) for x in range(4) for y in range(4) for z in range(4)][1:]
     trips.sort(key=lambda t: -sum(min(n, 4 - n) for n in t))
@@ -293,7 +298,7 @@
         out[2].start()
         out[3].start()
 
-    pl.semaphore_wait(inside, pats - 1)
+    pl.semaphore_wait(inside.at[1], 3)
     swap.wait()
     pgrad[half_of(core), :] += half[...]
     for n, trip in enumerate(trips):
@@ -355,7 +360,7 @@
             pltpu.VMEM(table.shape, jnp.bfloat16), vmem(2, 2, SIDE, HALF), vmem(2 * SIDE, SIDE),
             vmem(2, 2, 512, HALF), vmem(2, 2, HALF, 384),
             vmem(SIDE, SIDE), vmem(63, 8, HALF), vmem(2 * SIDE, SIDE),
-            dma(10), dma(10), dma(10), dma(7), dma(7), dma(4), dma(4), pltpu.SemaphoreType.REGULAR,
+            dma(10), dma(10), dma(10), dma(7), dma(7), dma(4), dma(4), pltpu.SemaphoreType.REGULAR((2,)),
         ],
         compiler_params=pltpu.CompilerParams(
             collective_id=0, has_side_effects=True, vmem_limit_bytes=56 * 2**20),

time: 67.6 us -> 66.4 us (0.982)
  Pallas kernels: 64.8 us -> 63.5 us
    pallas_call x1, Pallas kernels: 64.8 us -> 63.5 us  [on_device(): pl.pallas_call(functools.partial(kernel, tiles, pats), out_shape=[pltpu.V...]
where the time goes in v4:
time: 66.4 us; the launch traced here: 66.3 us
  Pallas kernels  63.5 us (96%)
  local copies, waits for them, and re-layouts  2.11 us (3%)
    pallas_call x1, Pallas kernels, on_device(): pl.pallas_call(functools.partial(kernel, tiles, pats), out_shape=[pltpu.V...  63.5 us
    unnamed x2, local copies, waits for them, and re-layouts  2.11 us

profile of v4, /device:TPU:1, one launch (start us, length us, event | category | flops | bytes accessed | tf_op | source)
XLA Modules:
  0.0 66.3 jit_solution(16418150066257628180)
XLA Ops:
  0.6 63.5 %shard_map.68 = (f32[2,2,512,256]{3,2,1,0:T(8,128)S(1)}, f32[2,256,256]{2,1,0:T(8,128)S(1)}) custom-call(s32[2,4]{1,0:T(2,128)} %bitcast.1, f32[2,2,512,256]{3,2,1,0:T(8,128)} %obj.1, f32[4,2,256,256]{3,2,1,0:T(8,128)} %meas_in.1, f32[2,256,256]{2,1,0:T(8,128)} %probe_in.1, bf16[21,256,256]{2,1,0:T(8,128)(2,1)} %constant.2.clone.tab_in), custom_call_target="tpu_custom_call" | custom-call | flops 27000000512 | bytes 10485760 | tf_op jit(solution)/shard_map/pallas_call | solution.py:353
  64.1 1.3 %copy.9 = f32[2,2,512,256]{3,2,1,0:T(8,128)} copy(f32[2,2,512,256]{3,2,1,0:T(8,128)S(1)} %get-tuple-element.2) | data formatting | bytes 4194304
  65.5 0.8 %copy.10 = f32[2,256,256]{2,1,0:T(8,128)} copy(f32[2,256,256]{2,1,0:T(8,128)S(1)} %get-tuple-element.3) | data formatting | bytes 1048576

commit v5 on v4

--- a/solution.py
+++ b/solution.py
@@ -299,7 +299,7 @@
         out[3].start()
 
     pl.semaphore_wait(inside.at[1], 3)
-    swap.wait()
+    swap.wait_recv()
     pgrad[half_of(core), :] += half[...]
     for n, trip in enumerate(trips):
         c, device = goal(trip)
@@ -341,6 +341,7 @@
     finish(3)
     finish(0)
     back.wait()
+    swap.wait_send()
 
 
 def on_device(scanned, measured, obj, probe):

time: 66.4 us -> 65.9 us (level)
  no operation moved by 1% of the time
where the time goes in v5:
time: 65.9 us; the launch traced here: 65.8 us
  Pallas kernels  63.1 us (96%)
  local copies, waits for them, and re-layouts  2.11 us (3%)
    pallas_call x1, Pallas kernels, on_device(): pl.pallas_call(functools.partial(kernel, tiles, pats), out_shape=[pltpu.V...  63.1 us
    unnamed x2, local copies, waits for them, and re-layouts  2.11 us

profile of v5, /device:TPU:1, one launch (start us, length us, event | category | flops | bytes accessed | tf_op | source)
XLA Modules:
  0.0 65.8 jit_solution(3201354643309810332)
XLA Ops:
  0.6 63.1 %shard_map.68 = (f32[2,2,512,256]{3,2,1,0:T(8,128)S(1)}, f32[2,256,256]{2,1,0:T(8,128)S(1)}) custom-call(s32[2,4]{1,0:T(2,128)} %bitcast.1, f32[2,2,512,256]{3,2,1,0:T(8,128)} %obj.1, f32[4,2,256,256]{3,2,1,0:T(8,128)} %meas_in.1, f32[2,256,256]{2,1,0:T(8,128)} %probe_in.1, bf16[21,256,256]{2,1,0:T(8,128)(2,1)} %constant.2.clone.tab_in), custom_call_target="tpu_custom_call" | custom-call | flops 27000000512 | bytes 10485760 | tf_op jit(solution)/shard_map/pallas_call | solution.py:354
  63.7 1.3 %copy.9 = f32[2,2,512,256]{3,2,1,0:T(8,128)} copy(f32[2,2,512,256]{3,2,1,0:T(8,128)S(1)} %get-tuple-element.2) | data formatting | bytes 4194304
  65.0 0.8 %copy.10 = f32[2,256,256]{2,1,0:T(8,128)} copy(f32[2,256,256]{2,1,0:T(8,128)S(1)} %get-tuple-element.3) | data formatting | bytes 1048576
